TPU v7x, 256 devices: a whole 4x4x8 slice. The times are simulated.
256 devices in a mesh: keys: 64 (over y, z, core), seq: 4 (over x).
Axes of the slice: x: 4, y: 4, z: 8, core: 2. Of those that a mesh axis runs over, the one named last changes fastest.
Arguments:
- span_queries: bfloat16 [1536, 768], P(('keys', 'seq')), may hold values from -6 to 6
- key_slab: bfloat16 [4096, 768], P('keys'), may hold values from -0.21875 to 0.21875
- neighbour_store: bfloat16 [4096, 64, 896], P('keys'), may hold values from -6 to 6
- neighbour_ids: int32 [1536, 2], P(('keys', 'seq')), may hold values from 0 to 4094, as said below
- attn_queries: bfloat16 [98304, 2048], P(('keys', 'seq')), may hold values from -200 to 200
- kv_weight: bfloat16 [2, 2048, 896], P(None, 'keys'), may hold values from -0.1875 to 0.1875
Outputs:
- best_scores: float32 [1536, 2], P(('keys', 'seq'))
- attended: bfloat16 [98304, 2048], P(('keys', 'seq'))
Inputs may be any that keep to these rules, and one draw needn't show every extreme that they name: `neighbour_ids`: each id c has c mod 64 at most 62, so c + 1 lies on the same shard c // 64. Among the 12 ids of one device's spans (aligned blocks of 6 rows), no shard holds more than 1, and some shard holds exactly 1.
All inputs are finite; a program needn't handle non-finite values.
Results may differ from a plain program's by a relative error of at most 0.012.
The roundings to bfloat16 on the way count: a program that leaves them out, or rounds other values in their place, can miss the bound.
Values may be sent and summed in bfloat16 or wider, within the bound.
A program may use at most 128 MiB of HBM per device.

v0:
```python
import jax
import jax.numpy as jnp
from jax import lax
from jax.sharding import PartitionSpec as P

HEADS = 16
HEAD_DIM = 128


def merged(part, axis, combine):
    gathered = jax.tree.map(lambda a: lax.all_gather(a, axis), part)

    def take(source):
        return jax.tree.map(lambda a: lax.dynamic_index_in_dim(a, source, 0, False), gathered)

    return lax.fori_loop(
        1, lax.axis_size(axis), lambda source, state: combine(state, take(source)), take(0)
    )


def keep_two(left, right):
    higher = jnp.maximum(left[0], right[0])
    runner = jnp.maximum(jnp.minimum(left[0], right[0]), jnp.maximum(left[1], right[1]))
    return (higher, runner)


def best_two(values):
    padding = jnp.full((values.shape[0], 2), -jnp.inf, values.dtype)
    return lax.top_k(jnp.concatenate([values, padding], axis=1), 2)[0]


def row_scores(left, right):
    return lax.dot_general(
        left, right, (((1,), (1,)), ((), ())), preferred_element_type=jnp.float32
    )


def body(span_queries, key_slab, neighbour_store, neighbour_ids, attn_queries, kv_weight):
    key_count = lax.axis_size("keys")
    position = lax.axis_index("keys")
    own_spans = neighbour_ids.shape[0]
    shard_spans = neighbour_store.shape[0]
    span_rows = neighbour_store.shape[1]
    enc_width = neighbour_store.shape[2]
    candidates = best_two(
        row_scores(lax.all_gather(span_queries, "keys", axis=0, tiled=True), key_slab)
    )
    higher_all, runner_all = merged((candidates[:, 0], candidates[:, 1]), "keys", keep_two)
    higher = lax.dynamic_slice_in_dim(higher_all, position * own_spans, own_spans)
    runner = lax.dynamic_slice_in_dim(runner_all, position * own_spans, own_spans)
    best_scores = jnp.stack([higher, runner], axis=1)
    flat_ids = neighbour_ids.reshape(-1)
    need_count = flat_ids.shape[0]
    per_shard = (need_count + key_count - 1) // key_count
    capacity = 2 * per_shard
    target = flat_ids // shard_spans
    offset = flat_ids % shard_spans
    order_index = jnp.arange(need_count, dtype=jnp.int32)
    same_shard = (target[:, None] == target[None, :]) & (
        order_index[:, None] < order_index[None, :]
    )
    slot_base = 2 * jnp.sum(same_shard.astype(jnp.int32), axis=0)
    slot_index = jnp.arange(capacity, dtype=jnp.int32)
    shard_onehot = (target[:, None] == jnp.arange(key_count, dtype=jnp.int32)[None, :]).astype(
        jnp.int32
    )
    first_slot = (slot_index == slot_base[..., None]).astype(jnp.int32) * offset[..., None]
    next_slot = (slot_index == slot_base[..., None] + 1).astype(jnp.int32) * (offset[..., None] + 1)
    table = jnp.einsum("nj,ns->js", shard_onehot, first_slot + next_slot)
    incoming = lax.all_to_all(table, "keys", split_axis=0, concat_axis=0, tiled=True)
    outgoing = neighbour_store[incoming]
    arrived = lax.all_to_all(outgoing, "keys", split_axis=0, concat_axis=0, tiled=True)
    arrived = arrived.reshape(key_count * capacity, span_rows, enc_width)
    first_row = target * capacity + slot_base
    picked = arrived[jnp.stack([first_row, first_row + 1], axis=1)]
    neighbours = picked.reshape(own_spans * 4 * span_rows, enc_width)
    keys_values = jnp.einsum(
        "re,tce->rtc",
        neighbours,
        lax.all_gather(kv_weight, "keys", axis=1, tiled=True),
        preferred_element_type=jnp.float32,
    ).astype(jnp.bfloat16)
    key_rows = keys_values[:, 0].reshape(own_spans, 4 * span_rows, HEADS, HEAD_DIM)
    value_rows = keys_values[:, 1].reshape(own_spans, 4 * span_rows, HEADS, HEAD_DIM)
    queries = attn_queries.reshape(own_spans, span_rows, HEADS, HEAD_DIM)
    logits = jnp.einsum(
        "cqhd,ckhd->chqk", queries, key_rows, preferred_element_type=jnp.float32
    ) * HEAD_DIM ** (-0.5)
    largest = jnp.max(logits, axis=-1, keepdims=True)
    expo_terms = jnp.exp(logits - largest)
    weights = (expo_terms / jnp.sum(expo_terms, axis=-1, keepdims=True)).astype(jnp.bfloat16)
    output = jnp.einsum("chqk,ckhd->cqhd", weights, value_rows, preferred_element_type=jnp.float32)
    attended = output.astype(jnp.bfloat16).reshape(own_spans * span_rows, HEADS * HEAD_DIM)
    return (best_scores, attended)


def solution(mesh):
    return jax.shard_map(
        body,
        mesh=mesh,
        in_specs=(
            P(("keys", "seq"), None),
            P("keys", None),
            P("keys", None, None),
            P(("keys", "seq"), None),
            P(("keys", "seq"), None),
            P(None, "keys", None),
        ),
        out_specs=(P(("keys", "seq"), None), P(("keys", "seq"), None)),
        check_vma=False,
    )
```

profile of v0, /device:TPU:1, one launch (start us, length us, event | category | flops | bytes accessed | tf_op | source)
XLA Modules:
  0.0 606.7 jit_solution(17030885371384447195)
XLA Ops:
  7.2 0.8 copy.33
  8.1 0.1 convert_reduce_fusion
  8.2 0.3 fusion.23
  8.5 22.2 %all_to_all.17 = s32[64,1,2]{2,1,0:T(1,128)S(1)} all-to-all(s32[64,1,2]{2,1,0:T(1,128)S(1)} %bitcast.81), channel_id=1, replica_groups=mesh['keys'=64,'seq'=4] {'keys'}, dimensions={0} | all-to-all | bytes 1024 | tf_op jit(solution)/shard_map/all_to_all | solution.py:70
  30.8 0.1 copy.36
  30.9 0.1 reshape.402
  31.1 11.9 %gather_fusion = bf16[128,64,896]{2,1,0:T(8,128)(2,1)} fusion(bf16[64,64,896]{2,1,0:T(8,128)(2,1)} %param.10, s32[1024]{0:T(1024)S(1)} %pad_clamp_fusion.1), kind=kCustom, calls=%fused_computation | custom fusion | bytes 29360640 | tf_op jit(solution)/shard_map/gather | solution.py:71
  43.0 6.2 %all-to-all-start.1 = ((bf16[64,2,64,896]{3,2,1,0:T(8,128)(2,1)}), bf16[64,2,64,896]{3,2,1,0:T(8,128)(2,1)}, u32[]{:S(2)}, u32[]{:S(2)}) async-start(bf16[64,2,64,896]{3,2,1,0:T(8,128)(2,1)} %bitcast.73), calls=%async_computation.1 | async-start | bytes 29360128 | tf_op jit(solution)/shard_map/all_to_all | solution.py:72
  49.3 0.7 all-gather.5.cloned.1.call-update
  50.1 0.1 copy.38
  50.3 1.6 copy.44
  51.8 380.2 %all-gather.2 = bf16[64,6,768]{2,1,0:T(8,128)(2,1)S(1)} all-gather(bf16[1,6,768]{2,1,0:T(8,128)(2,1)S(1)} %bitcast.82), channel_id=1, replica_groups=mesh['keys'=64,'seq'=4] {'keys'}, dimensions={0}, use_global_device_ids=true | all-gather | bytes 599040 | tf_op jit(solution)/shard_map/all_gather | solution.py:46
  432.0 0.2 reshape.426
  432.2 0.3 fusion.43
  432.5 5.0 top_k.8
  437.6 48.6 %all-gather = f32[24576,1]{0,1:T(1,128)S(1)} all-gather(f32[384,1]{0,1:T(1,128)S(1)} %get-tuple-element.161), channel_id=2, replica_groups=mesh['keys'=64,'seq'=4] {'keys'}, dimensions={0}, use_global_device_ids=true | all-gather | bytes 99840 | tf_op jit(solution)/shard_map/all_gather | solution.py:11
  486.2 0.5 broadcast.499
  486.7 0.9 reduce.14
  487.6 44.4 %all-gather.1 = f32[24576,1]{0,1:T(1,128)S(1)} all-gather(f32[384,1]{0,1:T(1,128)S(1)} %get-tuple-element.160), channel_id=3, replica_groups=mesh['keys'=64,'seq'=4] {'keys'}, dimensions={0}, use_global_device_ids=true | all-gather | bytes 99840 | tf_op jit(solution)/shard_map/all_gather | solution.py:11
  532.0 0.9 reduce.15
  533.0 4.3 while.17
  537.4 0.6 pad_maximum_fusion
  538.0 6.3 %gather_fusion.1 = bf16[24,64,896]{2,1,0:T(8,128)(2,1)S(1)} fusion(bf16[128,64,896]{2,1,0:T(8,128)(2,1)} %bitcast.6, s32[1024]{0:T(1024)S(1)} %pad_clamp_fusion), kind=kCustom, calls=%fused_computation.1 | custom fusion | bytes 5505120 | tf_op jit(solution)/shard_map/gather | solution.py:75
  544.3 18.7 %convolution_convert_fusion = bf16[1536,2,2048]{2,0,1:T(8,128)(2,1)} fusion(bf16[1536,896,1]{1,0,2:T(8,128)(2,1)S(1)} %bitcast.78, bf16[2,2048,896]{2,1,0:T(8,128)(2,1)} %all-gather.5.cloned.1.call-done), kind=kOutput, calls=%fused_computation.6 | convolution fusion | flops 11280580608 | bytes 22675456 | tf_op jit(solution)/shard_map/re,tce->rtc/dot_general | solution.py:77
  563.0 5.3 slice_bitcast_fusion.1
  568.3 2.3 copy.43
  570.7 3.7 fusion.5
  574.4 2.4 fusion.42
  576.8 5.0 copy.45
  581.8 15.5 %fusion.16 = bf16[6,64,16,128]{3,1,2,0:T(8,128)(2,1)S(1)} fusion(bf16[6,256,16,128]{3,2,1,0:T(8,128)(2,1)} %bitcast.75, f32[6,16,64]{2,1,0:T(8,128)S(1)} %fusion.42, f32[6,16,256,64]{2,3,1,0:T(8,128)} %copy-done.2), kind=kOutput, calls=%fused_computation.24 | convolution fusion | flops 411310336 | bytes 14180352 | tf_op jit(solution)/shard_map/chqk,ckhd->cqhd/dot_general | solution.py:92
  597.3 1.0 copy.42
  598.4 1.6 copy.58
  (158 shorter events, 3.2 us)
Async XLA Ops:
  7.2 425.0 %copy-start = (bf16[64,768]{1,0:T(8,128)(2,1)S(1)}, bf16[64,768]{1,0:T(8,128)(2,1)}, u32[]{:S(2)}) copy-start(bf16[64,768]{1,0:T(8,128)(2,1)} %param.9) | copy-start | bytes 294916
  43.0 7.3 %copy-start.3 = (bf16[384,2048]{1,0:T(8,128)(2,1)S(1)}, bf16[384,2048]{1,0:T(8,128)(2,1)}, u32[]{:S(2)}) copy-start(bf16[384,2048]{1,0:T(8,128)(2,1)} %param.12) | copy-start | bytes 4718596
  43.0 8.8 %copy-start.4 = (bf16[6,768]{1,0:T(8,128)(2,1)S(1)}, bf16[6,768]{1,0:T(8,128)(2,1)}, u32[]{:S(2)}) copy-start(bf16[6,768]{1,0:T(8,128)(2,1)} %param.8) | copy-start | bytes 27652
  43.0 495.0 %all-to-all-start.1 = ((bf16[64,2,64,896]{3,2,1,0:T(8,128)(2,1)}), bf16[64,2,64,896]{3,2,1,0:T(8,128)(2,1)}, u32[]{:S(2)}, u32[]{:S(2)}) async-start(bf16[64,2,64,896]{3,2,1,0:T(8,128)(2,1)} %bitcast.73), calls=%async_computation.1 | async-start | bytes 29360128 | tf_op jit(solution)/shard_map/all_to_all | solution.py:72
  49.2 495.1 %all-gather.5.cloned.1.call-start = ((), (), s32[]{:S(2)}) async-start(), calls=%async_computation.2 | async-start | bytes 7454720 | tf_op jit(solution)/shard_map/all_gather | solution.py:80
  574.4 7.4 %copy-start.2 = (f32[6,16,256,64]{2,3,1,0:T(8,128)}, f32[6,16,256,64]{2,3,1,0:T(8,128)S(1)}, u32[]{:S(2)}) copy-start(f32[6,16,256,64]{2,3,1,0:T(8,128)S(1)} %fusion.5) | copy-start | bytes 18874372
  581.8 18.1 %copy-start.1 = (bf16[64,768]{1,0:T(8,128)(2,1)S(1)}, bf16[64,768]{1,0:T(8,128)(2,1)}, u32[]{:S(2)}) copy-start(bf16[64,768]{1,0:T(8,128)(2,1)} %param.9) | copy-start | bytes 294916
Sparse Core Ops, SparseCore 0:
  52.8 128.8 all-gather.4
where the time goes:
time: 607 us
  blocking collectives  495 us (82%)
  local copies, waits for them, and re-layouts  39 us (6%)
  matrix products  38.6 us (6%)
  between operations  14.2 us (2%)
  other arithmetic  10.8 us (2%)
  starting transfers between devices  6.27 us (1%)
    all_gather x1, blocking collectives, body(): lax.all_gather(span_queries, 'keys', axis=0, tiled=True)  380 us
    all_gather x2, blocking collectives, merged(): gathered = jax.tree.map(lambda a: lax.all_gather(a, axis), part)  93 us
    all_to_all x1, blocking collectives, body(): lax.all_to_all(table, 'keys', split_axis=0, concat_axis=0, tiled=True)  22.2 us
    dot_general x1, matrix products, body(): jnp.einsum('re,tce->rtc', neighbours, lax.all_gather(kv_weight, 'keys', a...  18.7 us
    unnamed x17, local copies, waits for them, and re-layouts  16.8 us
    dot_general x1, matrix products, body(): jnp.einsum('chqk,ckhd->cqhd', weights, value_rows, preferred_element_type...  15.5 us
  transfers between devices with their start and end apart: 2, of which 0 were waited for; matrix products, arithmetic and copies ran while one was open for 3% of the time, Pallas kernels for 0%

commit v1 on v0

--- a/solution.py
+++ b/solution.py
@@ -42,9 +42,20 @@
     shard_spans = neighbour_store.shape[0]
     span_rows = neighbour_store.shape[1]
     enc_width = neighbour_store.shape[2]
-    candidates = best_two(
-        row_scores(lax.all_gather(span_queries, "keys", axis=0, tiled=True), key_slab)
-    )
+
+    def try_all_the_flows(chunk):
+        arr_next = jnp.concatenate(
+            lax.all_to_all(
+                jnp.stack([chunk] * lax.axis_size("keys")),
+                axis_name="keys",
+                concat_axis=0,
+                split_axis=0,
+            ),
+            axis=0,
+        )
+        return arr_next
+
+    candidates = best_two(row_scores(try_all_the_flows(span_queries), key_slab))
     higher_all, runner_all = merged((candidates[:, 0], candidates[:, 1]), "keys", keep_two)
     higher = lax.dynamic_slice_in_dim(higher_all, position * own_spans, own_spans)
     runner = lax.dynamic_slice_in_dim(runner_all, position * own_spans, own_spans)

time: 607 us -> 570 us (0.939)
  blocking collectives: 495 us -> 441 us
  waiting for transfers between devices: 0.7 us -> 11.5 us
    all_gather x1 -> x0, blocking collectives: 380 us -> none  [body(): lax.all_gather(span_queries, 'keys', axis=0, tiled=True)]
    all_gather x2, blocking collectives: 93 us -> 419 us  [merged(): gathered = jax.tree.map(lambda a: lax.all_gather(a, axis), part)]
    all_to_all x0 -> x1, waiting for transfers between devices: none -> 10.8 us  [try_all_the_flows(): lax.all_to_all(jnp.stack([chunk] * lax.axis_size('keys')), axis_name='key...]
    unnamed x17 -> x14, local copies, waits for them, and re-layouts: 16.8 us -> 16.6 us
  transfers between devices with their start and end apart: 2 -> 3, of which waited for: 0 -> 1; matrix products, arithmetic and copies ran while one was open for 3% -> 6% of each run, Pallas kernels for 0% -> 0%
where the time goes in v1:
time: 570 us
  blocking collectives  441 us (77%)
  local copies, waits for them, and re-layouts  40.7 us (7%)
  matrix products  38.6 us (7%)
  between operations  14.2 us (2%)
  waiting for transfers between devices  11.5 us (2%)
  starting transfers between devices  11.3 us (2%)
  other arithmetic  10.7 us (2%)
    all_gather x2, blocking collectives, merged(): gathered = jax.tree.map(lambda a: lax.all_gather(a, axis), part)  419 us
    all_to_all x1, blocking collectives, body(): lax.all_to_all(table, 'keys', split_axis=0, concat_axis=0, tiled=True)  22.2 us
    dot_general x1, matrix products, body(): jnp.einsum('re,tce->rtc', neighbours, lax.all_gather(kv_weight, 'keys', a...  18.7 us
    unnamed x14, local copies, waits for them, and re-layouts  16.6 us
    dot_general x1, matrix products, body(): jnp.einsum('chqk,ckhd->cqhd', weights, value_rows, preferred_element_type...  15.5 us
    gather x1, local copies, waits for them, and re-layouts, body(): outgoing = neighbour_store[incoming]  11.9 us
  transfers between devices with their start and end apart: 3, of which 1 were waited for; matrix products, arithmetic and copies ran while one was open for 6% of the time, Pallas kernels for 0%

profile of v1, /device:TPU:1, one launch (start us, length us, event | category | flops | bytes accessed | tf_op | source)
XLA Modules:
  0.0 569.7 jit_solution(4754678884196581791)
XLA Ops:
  7.2 0.8 copy.33
  8.2 0.3 fusion.23
  8.5 22.2 %all_to_all.22 = s32[64,1,2]{2,1,0:T(1,128)S(1)} all-to-all(s32[64,1,2]{2,1,0:T(1,128)S(1)} %bitcast.80), channel_id=1, replica_groups=mesh['keys'=64,'seq'=4] {'keys'}, dimensions={0} | all-to-all | bytes 1024 | tf_op jit(solution)/shard_map/all_to_all | solution.py:81
  30.7 1.6 stack.14
  32.4 4.7 all-to-all-start
  37.2 0.1 copy.36
  37.3 0.1 reshape.408
  37.5 11.9 %gather_fusion = bf16[128,64,896]{2,1,0:T(8,128)(2,1)} fusion(bf16[64,64,896]{2,1,0:T(8,128)(2,1)} %param.10, s32[1024]{0:T(1024)S(1)} %pad_clamp_fusion.1), kind=kCustom, calls=%fused_computation | custom fusion | bytes 29360640 | tf_op jit(solution)/shard_map/gather | solution.py:82
  49.4 10.8 %all-to-all-done = bf16[64,6,768]{2,1,0:T(8,128)(2,1)S(1)} async-done(((bf16[64,6,768]{2,1,0:T(8,128)(2,1)}), bf16[64,6,768]{2,1,0:T(8,128)(2,1)S(1)}, u32[]{:S(2)}, u32[]{:S(2)}) %all-to-all-start) | async-done | bytes 589856 | tf_op jit(solution)/shard_map/all_to_all | solution.py:48
  60.2 6.5 %all-to-all-start.2 = ((bf16[64,2,64,896]{3,2,1,0:T(8,128)(2,1)}), bf16[64,2,64,896]{3,2,1,0:T(8,128)(2,1)}, u32[]{:S(2)}, u32[]{:S(2)}) async-start(bf16[64,2,64,896]{3,2,1,0:T(8,128)(2,1)} %bitcast.72), calls=%async_computation.2 | async-start | bytes 29360128 | tf_op jit(solution)/shard_map/all_to_all | solution.py:83
  66.8 0.7 all-gather.4.cloned.1.call-update
  67.7 1.6 copy.44
  69.3 0.2 reshape.399
  69.5 0.3 fusion.43
  69.9 5.0 top_k.8
  74.9 372.3 %all-gather = f32[24576,1]{0,1:T(1,128)S(1)} all-gather(f32[384,1]{0,1:T(1,128)S(1)} %get-tuple-element.161), channel_id=2, replica_groups=mesh['keys'=64,'seq'=4] {'keys'}, dimensions={0}, use_global_device_ids=true | all-gather | bytes 99840 | tf_op jit(solution)/shard_map/all_gather | solution.py:11
  447.2 46.6 %all-gather.1 = f32[24576,1]{0,1:T(1,128)S(1)} all-gather(f32[384,1]{0,1:T(1,128)S(1)} %get-tuple-element.160), channel_id=3, replica_groups=mesh['keys'=64,'seq'=4] {'keys'}, dimensions={0}, use_global_device_ids=true | all-gather | bytes 99840 | tf_op jit(solution)/shard_map/all_gather | solution.py:11
  493.8 0.5 broadcast.501
  494.4 0.9 reduce.14
  495.2 0.9 reduce.15
  496.2 4.1 while.17
  500.4 0.6 pad_maximum_fusion
  500.9 6.3 %gather_fusion.1 = bf16[24,64,896]{2,1,0:T(8,128)(2,1)S(1)} fusion(bf16[128,64,896]{2,1,0:T(8,128)(2,1)} %bitcast.5, s32[1024]{0:T(1024)S(1)} %pad_clamp_fusion), kind=kCustom, calls=%fused_computation.1 | custom fusion | bytes 5505120 | tf_op jit(solution)/shard_map/gather | solution.py:86
  507.2 18.7 %convolution_convert_fusion = bf16[1536,2,2048]{2,0,1:T(8,128)(2,1)} fusion(bf16[1536,896,1]{1,0,2:T(8,128)(2,1)S(1)} %bitcast.77, bf16[2,2048,896]{2,1,0:T(8,128)(2,1)} %all-gather.4.cloned.1.call-done), kind=kOutput, calls=%fused_computation.6 | convolution fusion | flops 11280580608 | bytes 22675456 | tf_op jit(solution)/shard_map/re,tce->rtc/dot_general | solution.py:88
  526.0 5.3 slice_bitcast_fusion.1
  531.3 2.3 copy.43
  533.6 3.7 fusion.5
  537.3 2.4 fusion.42
  539.7 5.0 copy.45
  544.7 15.5 %fusion.16 = bf16[6,64,16,128]{3,1,2,0:T(8,128)(2,1)S(1)} fusion(bf16[6,256,16,128]{3,2,1,0:T(8,128)(2,1)} %bitcast.74, f32[6,16,64]{2,1,0:T(8,128)S(1)} %fusion.42, f32[6,16,256,64]{2,3,1,0:T(8,128)} %copy-done.2), kind=kOutput, calls=%fused_computation.24 | convolution fusion | flops 411310336 | bytes 14180352 | tf_op jit(solution)/shard_map/chqk,ckhd->cqhd/dot_general | solution.py:103
  560.3 1.0 copy.42
  561.3 1.6 copy.58
  (158 shorter events, 3.4 us)
Async XLA Ops:
  7.2 62.3 %copy-start = (bf16[64,768]{1,0:T(8,128)(2,1)S(1)}, bf16[64,768]{1,0:T(8,128)(2,1)}, u32[]{:S(2)}) copy-start(bf16[64,768]{1,0:T(8,128)(2,1)} %param.9) | copy-start | bytes 294916
  32.4 27.8 %all-to-all-start = ((bf16[64,6,768]{2,1,0:T(8,128)(2,1)}), bf16[64,6,768]{2,1,0:T(8,128)(2,1)S(1)}, u32[]{:S(2)}, u32[]{:S(2)}) async-start(bf16[64,6,768]{2,1,0:T(8,128)(2,1)} %stack.14), calls=%async_computation | async-start | bytes 1572864 | tf_op jit(solution)/shard_map/all_to_all | solution.py:48
  60.2 7.5 %copy-start.3 = (bf16[384,2048]{1,0:T(8,128)(2,1)S(1)}, bf16[384,2048]{1,0:T(8,128)(2,1)}, u32[]{:S(2)}) copy-start(bf16[384,2048]{1,0:T(8,128)(2,1)} %param.12) | copy-start | bytes 4718596
  60.2 440.7 %all-to-all-start.2 = ((bf16[64,2,64,896]{3,2,1,0:T(8,128)(2,1)}), bf16[64,2,64,896]{3,2,1,0:T(8,128)(2,1)}, u32[]{:S(2)}, u32[]{:S(2)}) async-start(bf16[64,2,64,896]{3,2,1,0:T(8,128)(2,1)} %bitcast.72), calls=%async_computation.2 | async-start | bytes 29360128 | tf_op jit(solution)/shard_map/all_to_all | solution.py:83
  66.7 440.5 %all-gather.4.cloned.1.call-start = ((), (), s32[]{:S(2)}) async-start(), calls=%async_computation.3 | async-start | bytes 7454720 | tf_op jit(solution)/shard_map/all_gather | solution.py:91
  537.3 7.4 %copy-start.2 = (f32[6,16,256,64]{2,3,1,0:T(8,128)}, f32[6,16,256,64]{2,3,1,0:T(8,128)S(1)}, u32[]{:S(2)}) copy-start(f32[6,16,256,64]{2,3,1,0:T(8,128)S(1)} %fusion.5) | copy-start | bytes 18874372
  544.7 18.1 %copy-start.1 = (bf16[64,768]{1,0:T(8,128)(2,1)S(1)}, bf16[64,768]{1,0:T(8,128)(2,1)}, u32[]{:S(2)}) copy-start(bf16[64,768]{1,0:T(8,128)(2,1)} %param.9) | copy-start | bytes 294916
Sparse Core Ops, SparseCore 0:
  70.3 128.2 all-gather.3
